TPU v7x, 32 devices: a whole 2x2x4 slice. The times are simulated.
32 devices in a mesh: kpt: 2 (over y), band: 4 (over x, core), slab: 4 (over z).
Axes of the slice: x: 2, y: 2, z: 4, core: 2. Of those that a mesh axis runs over, the one named last changes fastest.
Arguments:
- wavefunctions: bfloat16 [4, 256, 4, 64, 128], P('band', 'kpt', None, 'slab'), parts along dimension 1, may hold values from -6 to 6
- projectors: bfloat16 [4, 4, 96, 8, 18, 128], P('band', 'slab'), may hold values from -0.09375 to 0.09375
- block_index: int32 [4, 4, 96, 8], P('band', 'slab'), may hold values from -1 to 15, as said below
- proj_counts: int32 [4, 96], P('band'), may hold values from 6 to 18, as said below
- coupling: bfloat16 [4, 96, 18, 18], P('band'), may hold values from -4 to 4
- potential: bfloat16 [4, 64, 128], P('band', 'slab'), may hold values from -1 to 1
Outputs:
- applied: bfloat16 [4, 256, 4, 64, 128], P('band', 'kpt', None, 'slab'), parts along dimension 1
There are 2 independent parts, one for each index of `kpt`. A program takes and returns all parts, laid end to end along the dimension named above; an argument that names none is the same for every part. Nothing has to cross between parts.
Inputs may be any that keep to these rules, and one draw needn't show every extreme that they name: `block_index`: for each region, slab and atom the used slots come first and name distinct blocks; -1 marks an unused slot; every atom uses at least one slot on every slab. `proj_counts`: some atom of every region uses all 18 projectors.
All inputs are finite; a program needn't handle non-finite values.
Results may differ from a plain program's by a relative error of at most 0.0046.
Values may be sent and summed in bfloat16 or wider, within the bound.
A program may use at most 128 MiB of HBM per device.

v0:
```python
import jax
import jax.numpy as jnp
from jax import lax
from jax.sharding import PartitionSpec as P

NPROJ = 18
AT = 96
BLK = 16
CELLS = 128


def build_table(proj_values, slot_blocks, used_counts):
    onehot = (slot_blocks[..., None] == jnp.arange(BLK, dtype=jnp.int32)).astype(jnp.bfloat16)
    keep = (jnp.arange(NPROJ, dtype=jnp.int32)[None, None, :] < used_counts[:, :, None]).astype(
        jnp.float32
    )
    table = jnp.einsum("rajb,rajkp->rakbp", onehot, proj_values, preferred_element_type=jnp.float32)
    table = (table * keep[..., None, None]).astype(jnp.bfloat16)
    return table.reshape(table.shape[0], AT * NPROJ, BLK * CELLS)


def couple_terms(coeffs, coupling):
    regions_here = coeffs.shape[0]
    columns = coeffs.shape[2]
    shaped = coeffs.reshape(regions_here, AT, NPROJ, columns)
    mixed = jnp.einsum(
        "raij,rajn->rain", coupling.astype(jnp.float32), shaped, precision=lax.Precision.HIGHEST
    )
    return mixed.reshape(regions_here, AT * NPROJ, columns).astype(jnp.bfloat16)


def apply_part(psi_rows, table, coupling, potential_rows):
    coeffs = jnp.einsum("rkp,rnp->rkn", table, psi_rows, preferred_element_type=jnp.float32)
    summed = lax.psum(coeffs, "slab")
    coupled = couple_terms(summed, coupling)
    nonlocal_part = jnp.einsum("rkn,rkp->rnp", coupled, table, preferred_element_type=jnp.float32)
    local_part = potential_rows.astype(jnp.float32)[:, None, :] * psi_rows.astype(jnp.float32)
    return (local_part + nonlocal_part).astype(jnp.bfloat16)


def on_device(wavefunctions, projectors, block_index, proj_counts, coupling, potential):
    table = build_table(projectors[:, 0], block_index[:, 0], proj_counts)
    potential_rows = potential.reshape(1, BLK * CELLS)
    received = lax.all_to_all(wavefunctions, "band", split_axis=2, concat_axis=0, tiled=True)
    group_count = received.shape[0]
    members = received.shape[1]
    psi_rows = received.reshape(1, group_count * members, BLK * CELLS)
    result = apply_part(psi_rows, table, coupling, potential_rows)
    result = result.reshape(group_count, members, 1, BLK, CELLS)
    return lax.all_to_all(result, "band", split_axis=0, concat_axis=2, tiled=True)


def solution(mesh):
    in_specs = (
        P("band", "kpt", None, "slab", None),
        P("band", "slab", None, None, None, None),
        P("band", "slab", None, None),
        P("band", None),
        P("band", None, None, None),
        P("band", "slab", None),
    )
    out_specs = P("band", "kpt", None, "slab", None)
    return jax.shard_map(
        on_device, mesh=mesh, in_specs=in_specs, out_specs=out_specs, check_vma=False
    )
```

profile of v0, /device:TPU:0, one launch (start us, length us, event | category | flops | bytes accessed | tf_op | source)
XLA Modules:
  0.0 285.0 jit_solution(5553644044322625413)
XLA Ops:
  6.5 0.0 copy-start
  6.5 0.0 copy-start.2
  6.5 0.0 copy-start.3
  6.5 3.4 %copy.15 = bf16[1,128,4,16,128]{4,3,1,0,2:T(8,128)(2,1)} copy(bf16[1,128,4,16,128]{4,3,2,1,0:T(8,128)(2,1)} %param.6) | data formatting | bytes 4194304 | tf_op args[0]
  10.0 4.4 %all-to-all-start = ((bf16[1,128,4,16,128]{4,3,1,0,2:T(8,128)(2,1)}), bf16[1,128,4,16,128]{4,3,1,0,2:T(8,128)(2,1)}, u32[]{:S(2)}, u32[]{:S(2)}) async-start(bf16[1,128,4,16,128]{4,3,1,0,2:T(8,128)(2,1)} %copy.15), calls=%async_computation | async-start | bytes 4194304 | tf_op jit(solution)/shard_map/all_to_all | solution.py:44
  14.4 0.0 all-reduce.2.cloned.1.call-start
  14.5 0.0 copy-done.2
  14.5 0.7 copy.16
  15.2 0.0 copy-done.3
  15.2 0.1 fusion.18
  15.3 0.0 copy-done
  15.3 7.3 %fusion = bf16[1,96,18,128,16]{3,4,2,1,0:T(8,128)(2,1)} fusion(f32[96,18]{1,0:T(8,128)S(1)} %fusion.18, bf16[1,1,96,8,18,128]{5,3,4,2,1,0:T(8,128)(2,1)S(1)} %copy-done, s32[96,8]{1,0:T(8,128)} %copy.16), kind=kOutput, calls=%fused_computation.1 | convolution fusion | flops 63713280 | bytes 10626816 | tf_op jit(solution)/shard_map/rajb,rajkp->rakbp/dot_general | solution.py:17
  22.5 18.2 %all-to-all-done = bf16[1,128,4,16,128]{4,3,1,0,2:T(8,128)(2,1)} async-done(((bf16[1,128,4,16,128]{4,3,1,0,2:T(8,128)(2,1)}), bf16[1,128,4,16,128]{4,3,1,0,2:T(8,128)(2,1)}, u32[]{:S(2)}, u32[]{:S(2)}) %all-to-all-start) | async-done | bytes 2097184 | tf_op jit(solution)/shard_map/all_to_all | solution.py:44
  40.8 9.3 %fusion.3 = f32[1728,512]{1,0:T(8,128)} fusion(bf16[216,8,16,128]{3,2,1,0:T(8,128)(2,1)} %bitcast.63, bf16[64,8,16,128]{3,2,1,0:T(8,128)(2,1)} %bitcast.25), kind=kOutput, calls=%fused_computation.4 | convolution fusion | flops 3623878656 | bytes 12713984 | tf_op jit(solution)/shard_map/rkp,rnp->rkn/dot_general | solution.py:33
  50.1 4.8 %reshape.102 = f32[96,18,512]{2,1,0:T(8,128)} reshape(f32[1728,512]{1,0:T(8,128)} %fusion.3) | data formatting | bytes 7077888 | tf_op jit(solution)/shard_map/reshape.20
  54.9 0.0 copy-start.1
  54.9 0.0 all-reduce.2.cloned.1.call-update
  55.0 2.0 copy.17
  57.0 0.0 copy-done.1
  57.0 171.2 %all-reduce.2.cloned.1.call-done = f32[96,18,512]{2,1,0:T(8,128)} async-done(((f32[96,18,512]{2,1,0:T(8,128)}), f32[96,18,512]{2,1,0:T(8,128)}) %all-reduce.2.cloned.1.call-update) | async-done | bytes 3538960 | tf_op jit(solution)/shard_map/psum | solution.py:34
  228.2 6.6 %convert_bitcast_fusion = bf16[96,18,512]{2,1,0:T(8,128)(2,1)} fusion(f32[96,18,512]{2,1,0:T(8,128)} %all-reduce.2.cloned.1.call-done, bf16[96,18,18]{2,1,0:T(8,128)(2,1)} %copy.17), kind=kOutput, calls=%fused_computation.10 | convolution fusion | flops 191987712 | bytes 5370624 | tf_op jit(solution)/shard_map/raij,rajn->rain/dot_general | solution.py:26
  234.8 3.8 %convert_element_type.57 = bf16[1728,512]{1,0:T(8,128)(2,1)} reshape(bf16[96,18,512]{2,1,0:T(8,128)(2,1)} %convert_bitcast_fusion) | data formatting | bytes 3538944 | tf_op jit(solution)/shard_map/convert_element_type | solution.py:29
  238.6 8.7 %fusion.12 = bf16[64,8,16,128]{3,1,2,0:T(8,128)(2,1)S(1)} fusion(bf16[1728,512]{1,0:T(8,128)(2,1)} %convert_element_type.57, bf16[216,8,16,128]{3,2,1,0:T(8,128)(2,1)} %bitcast.64, bf16[64,8,16,128]{3,2,1,0:T(8,128)(2,1)} %bitcast.25, f32[2048]{0:T(1024)S(1)} %bitcast_convert_fusion), kind=kOutput, calls=%fused_computation.13 | convolution fusion | flops 3628072960 | bytes 13049856 | tf_op jit(solution)/shard_map/rkn,rkp->rnp/dot_general | solution.py:36
  247.3 0.6 copy.23
  247.9 28.3 %all_to_all.33 = bf16[4,128,1,16,128]{4,3,1,2,0:T(8,128)(2,1)S(1)} all-to-all(bf16[4,128,1,16,128]{4,3,1,2,0:T(8,128)(2,1)S(1)} %bitcast.61), channel_id=1, replica_groups=mesh['kpt'=2,'band'=4,'slab'=4] {'band'}, dimensions={0} | all-to-all | bytes 4194304 | tf_op jit(solution)/shard_map/all_to_all | solution.py:50
  276.2 2.0 copy.19
  (1 shorter events, 0.0 us)
Async XLA Ops:
  6.5 8.7 %copy-start = (bf16[1,1,96,8,18,128]{5,3,4,2,1,0:T(8,128)(2,1)S(1)}, bf16[1,1,96,8,18,128]{5,3,4,2,1,0:T(8,128)(2,1)}, u32[]{:S(2)}) copy-start(bf16[1,1,96,8,18,128]{5,3,4,2,1,0:T(8,128)(2,1)} %param.7) | copy-start | bytes 10616836
  6.5 7.9 %copy-start.2 = (s32[1,1,96,8]{2,3,1,0:T(8,128)S(1)}, s32[1,1,96,8]{2,3,1,0:T(8,128)}, u32[]{:S(2)}) copy-start(s32[1,1,96,8]{2,3,1,0:T(8,128)} %param.8) | copy-start | bytes 9220
  6.5 8.6 %copy-start.3 = (s32[1,96]{1,0:T(1,128)S(1)}, s32[1,96]{1,0:T(1,128)}, u32[]{:S(2)}) copy-start(s32[1,96]{1,0:T(1,128)} %param.9) | copy-start | bytes 1156
  10.0 30.8 %all-to-all-start = ((bf16[1,128,4,16,128]{4,3,1,0,2:T(8,128)(2,1)}), bf16[1,128,4,16,128]{4,3,1,0,2:T(8,128)(2,1)}, u32[]{:S(2)}, u32[]{:S(2)}) async-start(bf16[1,128,4,16,128]{4,3,1,0,2:T(8,128)(2,1)} %copy.15), calls=%async_computation | async-start | bytes 4194304 | tf_op jit(solution)/shard_map/all_to_all | solution.py:44
  14.4 213.8 %all-reduce.2.cloned.1.call-start = ((), (), s32[]{:S(2)}) async-start(), calls=%async_computation.2 | async-start | bytes 9437184 | tf_op jit(solution)/shard_map/psum | solution.py:34
  54.9 2.1 copy-start.1
Sparse Core Ops, SparseCore 0:
  55.1 173.0 all-reduce.1
where the time goes:
time: 285 us
  waiting for transfers between devices  189 us (66%)
  matrix products  31.8 us (11%)
  blocking collectives  28.3 us (10%)
  local copies, waits for them, and re-layouts  17.4 us (6%)
  between operations  13.5 us (5%)
  starting transfers between devices  4.49 us (2%)
    psum x1, waiting for transfers between devices, apply_part(): summed = lax.psum(coeffs, 'slab')  171 us
    all_to_all x1, blocking collectives, on_device(): lax.all_to_all(result, 'band', split_axis=0, concat_axis=2, tiled=True)  28.3 us
    all_to_all x1, waiting for transfers between devices, on_device(): lax.all_to_all(wavefunctions, 'band', split_axis=2, concat_axis=0, tiled=...  18.2 us
    dot_general x1, matrix products, apply_part(): jnp.einsum('rkp,rnp->rkn', table, psi_rows, preferred_element_type=jnp.fl...  9.34 us
    dot_general x1, matrix products, apply_part(): jnp.einsum('rkn,rkp->rnp', coupled, table, preferred_element_type=jnp.flo...  8.65 us
    dot_general x1, matrix products, build_table(): jnp.einsum('rajb,rajkp->rakbp', onehot, proj_values, preferred_element_ty...  7.26 us
    another operation x2, local copies, waits for them, and re-layouts  6.85 us
    dot_general x1, matrix products, couple_terms(): jnp.einsum('raij,rajn->rain', coupling.astype(jnp.float32), shaped, preci...  6.58 us
  transfers between devices with their start and end apart: 2, of which 2 were waited for; matrix products, arithmetic and copies ran while one was open for 4% of the time, Pallas kernels for 0%

commit v1 on v0

v1 whole, which is shorter than its diff:
```python
import functools

import jax
import jax.numpy as jnp
from jax import lax
from jax.experimental import pallas as pl
from jax.experimental.pallas import tpu as pltpu
from jax.sharding import PartitionSpec as P

MESH = pl.DeviceIdType.MESH


def partner(g, d):
    out, bit = g, 1
    while bit <= d:
        if d & bit:
            out = out + bit - 2 * bit * lax.rem(lax.div(g, bit), 2)
        bit *= 2
    return out


def kernel(dims, psi_ref, proj_ref, idx_ref, cmat_ref, pot_ref, out_ref,
           table, psir, res, part, from_left, from_right, total, mixed, cwide, coupled, flipped,
           psi_send, psi_recv, out_send, out_recv, rs_send, left_recv, right_recv,
           ag_send_r, ag_send_l, ag_recv):
    G, S, NP, AIN, SL, NB, NCH, m = dims
    rows_o = NP * AIN
    rows = S * rows_o
    gpc = G // NCH
    width = gpc * m
    g = lax.axis_index("band")
    s = lax.axis_index("slab")

    barrier = pltpu.get_barrier_semaphore()
    for d in range(1, G):
        pl.semaphore_signal(barrier, inc=1, device_id={"band": partner(g, d)}, device_id_type=MESH)

    @pl.when(s > 0)
    def _():
        pl.semaphore_signal(barrier, inc=1, device_id={"slab": s - 1}, device_id_type=MESH)

    @pl.when(s < S - 1)
    def _():
        pl.semaphore_signal(barrier, inc=1, device_id={"slab": s + 1}, device_id_type=MESH)

    ends = jnp.where(s > 0, 1, 0) + jnp.where(s < S - 1, 1, 0)
    pl.semaphore_wait(barrier, G - 1 + ends)

    def psi_copy(d):
        return pltpu.make_async_remote_copy(
            src_ref=psi_ref.at[partner(g, d)], dst_ref=psir.at[d],
            send_sem=psi_send.at[d], recv_sem=psi_recv.at[d],
            device_id={"band": partner(g, d)}, device_id_type=MESH)

    def out_copy(d):
        return pltpu.make_async_remote_copy(
            src_ref=res.at[d], dst_ref=out_ref.at[g],
            send_sem=out_send.at[d], recv_sem=out_recv.at[d],
            device_id={"band": partner(g, d)}, device_id_type=MESH)

    def rs_copy(c, o, right):
        return pltpu.make_async_remote_copy(
            src_ref=part.at[c, o], dst_ref=(from_left if right else from_right).at[c, o],
            send_sem=rs_send.at[c, o], recv_sem=(left_recv if right else right_recv).at[c, o],
            device_id={"slab": s + 1 if right else s - 1}, device_id_type=MESH)

    def ag_copy(c, o, right):
        return pltpu.make_async_remote_copy(
            src_ref=coupled.at[c, o], dst_ref=coupled.at[c, o],
            send_sem=(ag_send_r if right else ag_send_l).at[c, o], recv_sem=ag_recv.at[c, o],
            device_id={"slab": s + 1 if right else s - 1}, device_id_type=MESH)

    for d in range(1, G):
        psi_copy(d).start()
    psir[0] = psi_ref[g]

    def build(t, carry):
        at = pl.ds(pl.multiple_of(t * 16, 16), 16)
        where_to = idx_ref[at, :]
        slots = [jnp.broadcast_to(where_to[:, j:j + 1], (16, 128)) for j in range(SL)]
        values = [proj_ref[j, at, :].astype(jnp.float32) for j in range(SL)]
        for b in range(NB):
            acc = jnp.zeros((16, 128), jnp.float32)
            for j in range(SL):
                acc = jnp.where(slots[j] == b, values[j], acc)
            table[at, b * 128:(b + 1) * 128] = acc.astype(jnp.bfloat16)
        return carry

    lax.fori_loop(0, rows // 16, build, 0)

    def project(c):
        for d in range(c * gpc, (c + 1) * gpc):
            if d > 0:
                psi_copy(d).wait_recv()

        def one(o, carry):
            at = pl.ds(pl.multiple_of(o * rows_o, rows_o), rows_o)
            psi = psir[c * gpc:(c + 1) * gpc].reshape(width, NB * 128)
            value = lax.dot_general(table[at, :], psi, (((1,), (1,)), ((), ())),
                                    preferred_element_type=jnp.float32)
            part[c, o] = value.astype(jnp.bfloat16)

            @pl.when(o == s)
            def _():
                total[c] = value
            return carry

        lax.fori_loop(0, S, one, 0)

        @pl.when(s == 0)
        def _():
            for o in range(S - 1, 0, -1):
                rs_copy(c, o, True).start()

        @pl.when(s == S - 1)
        def _():
            for o in range(S - 1):
                rs_copy(c, o, False).start()

    def add_in(c, o, box):
        part[c, o] = (part[c, o].astype(jnp.float32) + box[c, o].astype(jnp.float32)).astype(jnp.bfloat16)

    def reduce_on(c):
        for i in range(S - 2):
            o = S - 1 - i

            @pl.when((s > 0) & (s < o))
            def _():
                rs_copy(c, o, True).wait_recv()
                add_in(c, o, from_left)
                rs_copy(c, o, True).start()

            @pl.when((s < S - 1) & (s > i))
            def _():
                rs_copy(c, i, False).wait_recv()
                add_in(c, i, from_right)
                rs_copy(c, i, False).start()

        @pl.when(s > 0)
        def _():
            rs_copy(c, s, True).wait_recv()
            total[c] += from_left[c, s].astype(jnp.float32)

        @pl.when(s < S - 1)
        def _():
            rs_copy(c, s, False).wait_recv()
            total[c] += from_right[c, s].astype(jnp.float32)

        def mix(i, carry):
            acc = jnp.zeros((AIN, width), jnp.float32)
            for j in range(NP):
                acc += cwide[i * NP + j] * total[c, j * AIN:(j + 1) * AIN, :]
            mixed[pl.ds(pl.multiple_of(i * AIN, AIN), AIN), :] = acc
            return carry

        lax.fori_loop(0, NP, mix, 0)
        coupled[c, s] = mixed[...].astype(jnp.bfloat16)

        @pl.when(s < S - 1)
        def _():
            ag_copy(c, s, True).start()

        @pl.when(s > 0)
        def _():
            ag_copy(c, s, False).start()

    def gather_on(c):
        for i in range(1, S):
            @pl.when(s - i >= 0)
            def _():
                ag_copy(c, s - i, True).wait_recv()

                @pl.when(s < S - 1)
                def _():
                    ag_copy(c, s - i, True).start()

            @pl.when(s + i < S)
            def _():
                ag_copy(c, s + i, False).wait_recv()

                @pl.when(s > 0)
                def _():
                    ag_copy(c, s + i, False).start()

    def apply(c):
        flipped[...] = coupled[c].reshape(rows, width).T
        step = 256

        def one(q, carry):
            at = pl.ds(pl.multiple_of(q * step, step), step)
            psi = psir[c * gpc:(c + 1) * gpc, :, at].reshape(width, step)
            value = jnp.dot(flipped[...], table[:, at], preferred_element_type=jnp.float32)
            value += pot_ref[:, at] * psi.astype(jnp.float32)
            value = value.astype(jnp.bfloat16).reshape(gpc, m, step)
            res[c * gpc:(c + 1) * gpc, :, at] = value
            return carry

        lax.fori_loop(0, NB * 128 // step, one, 0)
        for d in range(c * gpc, (c + 1) * gpc):
            if d > 0:
                out_copy(d).start()
            else:
                out_ref[g] = res[0]

    project(0)
    if NCH > 1:
        project(1)
    for ij in range(NP * NP):
        cwide[ij] = jnp.broadcast_to(cmat_ref[:, ij:ij + 1], (AIN, width))
    for c in range(NCH):
        reduce_on(c)
        if c >= 1:
            if c + 1 < NCH:
                project(c + 1)
            gather_on(c - 1)
            apply(c - 1)
    gather_on(NCH - 1)
    apply(NCH - 1)

    for d in range(1, G):
        psi_copy(d).wait_send()
        out_copy(d).wait_send()
        out_copy(d).wait_recv()
    for c in range(NCH):
        for o in range(S):
            @pl.when(s != o)
            def _():
                rs_copy(c, o, True).wait_send()

            @pl.when((s < S - 1) & (s >= o))
            def _():
                ag_copy(c, o, True).wait_send()

            @pl.when((s > 0) & (s <= o))
            def _():
                ag_copy(c, o, False).wait_send()


def on_device(G, S, wavefunctions, projectors, block_index, proj_counts, coupling, potential):
    _, m, regions, NB, cells = wavefunctions.shape
    _, _, AT, SL, NP, _ = projectors.shape
    own = AT // S
    AIN = -(-own // 8) * 8
    NCH = min(4, G)
    rows = S * NP * AIN
    gpc = G // NCH
    width = gpc * m
    s = lax.axis_index("slab")
    psi = jnp.transpose(wavefunctions[0].reshape(m, regions, NB * cells), (1, 0, 2))
    proj = projectors[0, 0].reshape(S, own, SL, NP, cells).transpose(2, 0, 3, 1, 4)
    proj = jnp.pad(proj, ((0, 0), (0, 0), (0, 0), (0, AIN - own), (0, 0))).reshape(SL, rows, cells)
    used = jnp.arange(NP, dtype=jnp.int32)[None, :, None, None] < proj_counts[0].reshape(S, 1, own, 1)
    idx = jnp.where(used, block_index[0, 0].reshape(S, 1, own, SL), -1)
    idx = jnp.pad(idx, ((0, 0), (0, 0), (0, AIN - own), (0, 0)), constant_values=-1).reshape(rows, SL)
    idx = jnp.pad(idx, ((0, 0), (0, 128 - SL)), constant_values=-1)
    cmat = lax.dynamic_slice_in_dim(coupling[0].reshape(AT, NP * NP), s * own, own, 0).astype(jnp.float32)
    cmat = jnp.pad(cmat, ((0, AIN - own), (0, (-NP * NP) % 128)))
    pot = potential.reshape(1, NB * cells).astype(jnp.float32)
    bf = jnp.bfloat16
    rows_o = NP * AIN
    dma = pltpu.SemaphoreType.DMA
    vmem = pl.BlockSpec(memory_space=pltpu.VMEM)
    out = pl.pallas_call(
        functools.partial(kernel, (G, S, NP, AIN, SL, NB, NCH, m)),
        out_shape=jax.ShapeDtypeStruct((G, m, NB * cells), bf),
        in_specs=[vmem] * 5,
        out_specs=vmem,
        scratch_shapes=[
            pltpu.VMEM((rows, NB * cells), bf),
            pltpu.VMEM((G, m, NB * cells), bf),
            pltpu.VMEM((G, m, NB * cells), bf),
            pltpu.VMEM((NCH, S, rows_o, width), bf),
            pltpu.VMEM((NCH, S, rows_o, width), bf),
            pltpu.VMEM((NCH, S, rows_o, width), bf),
            pltpu.VMEM((NCH, rows_o, width), jnp.float32),
            pltpu.VMEM((rows_o, width), jnp.float32),
            pltpu.VMEM((NP * NP, AIN, width), jnp.float32),
            pltpu.VMEM((NCH, S, rows_o, width), bf),
            pltpu.VMEM((width, rows), bf),
            dma((G,)), dma((G,)), dma((G,)), dma((G,)),
            dma((NCH, S)), dma((NCH, S)), dma((NCH, S)),
            dma((NCH, S)), dma((NCH, S)), dma((NCH, S)),
        ],
        compiler_params=pltpu.CompilerParams(
            collective_id=0, has_side_effects=True, vmem_limit_bytes=56 * 1024 * 1024),
        cost_estimate=pl.CostEstimate(
            flops=4 * rows * NB * cells * width * NCH, bytes_accessed=16 << 20, transcendentals=0),
    )(psi, proj, idx, cmat, pot)
    out = jnp.transpose(out, (1, 0, 2)).reshape(1, m, regions, NB, cells)
    return out


def solution(mesh):
    in_specs = (
        P("band", "kpt", None, "slab", None),
        P("band", "slab", None, None, None, None),
        P("band", "slab", None, None),
        P("band", None),
        P("band", None, None, None),
        P("band", "slab", None),
    )
    out_specs = P("band", "kpt", None, "slab", None)
    return jax.shard_map(
        functools.partial(on_device, mesh.shape["band"], mesh.shape["slab"]),
        mesh=mesh, in_specs=in_specs, out_specs=out_specs, check_vma=False)
```

time: 285 us -> 147 us (0.52)
  waiting for transfers between devices: 189 us -> 0 us
  Pallas kernels: 0 us -> 128 us
  matrix products: 31.8 us -> 0 us
  blocking collectives: 28.3 us -> 0 us
  between operations: 13.5 us -> 0.06 us
  starting transfers between devices: 4.49 us -> 0 us
  other arithmetic: 0.08 us -> 3.54 us
    psum x1 -> x0, waiting for transfers between devices: 171 us -> none  [apply_part(): summed = lax.psum(coeffs, 'slab')]
    pallas_call x0 -> x1, Pallas kernels: none -> 128 us  [on_device(): pl.pallas_call(functools.partial(kernel, (G, S, NP, AIN, SL, NB, NCH, m))...]
    dot_general x4 -> x0, matrix products: 31.8 us -> none  [the longest x1 9.34 us: apply_part(): jnp.einsum('rkp,rnp->rkn', table, psi_rows, preferred_element_type=jnp.fl...]
    all_to_all x1 -> x0, blocking collectives: 28.3 us -> none  [on_device(): lax.all_to_all(result, 'band', split_axis=0, concat_axis=2, tiled=True)]
    all_to_all x1 -> x0, waiting for transfers between devices: 18.2 us -> none  [on_device(): lax.all_to_all(wavefunctions, 'band', split_axis=2, concat_axis=0, tiled=...]
    all_to_all x1 -> x0, starting transfers between devices: 4.45 us -> none  [on_device(): lax.all_to_all(wavefunctions, 'band', split_axis=2, concat_axis=0, tiled=...]
    convert_element_type x1 -> x0, local copies, waits for them, and re-layouts: 3.82 us -> none  [couple_terms(): return mixed.reshape(regions_here, AT * NPROJ, columns).astype(jnp.bfloat16)]
    another operation x2 -> x4, local copies, waits for them, and re-layouts: 6.85 us -> 8.61 us  [the longest x2 5.01 us: on_device(): wavefunctions[0].reshape(m, regions, NB * cells)]
  transfers between devices with their start and end apart: 2 -> 0, of which waited for: 2 -> 0; matrix products, arithmetic and copies ran while one was open for 4% -> 0% of each run, Pallas kernels for 0% -> 0%
where the time goes in v1:
time: 147 us
  Pallas kernels  128 us (87%)
  local copies, waits for them, and re-layouts  15.4 us (10%)
  other arithmetic  3.54 us (2%)
    pallas_call x1, Pallas kernels, on_device(): pl.pallas_call(functools.partial(kernel, (G, S, NP, AIN, SL, NB, NCH, m))...  128 us
    another operation x2, local copies, waits for them, and re-layouts, on_device(): wavefunctions[0].reshape(m, regions, NB * cells)  5.01 us

profile of v1, /device:TPU:0, one launch (start us, length us, event | category | flops | bytes accessed | tf_op | source)
XLA Modules:
  0.0 147.1 jit_solution(11136611400101279277)
XLA Ops:
  0.0 0.5 broadcast.21
  0.5 1.3 reduce.3
  1.8 0.1 lt.27
  1.9 1.3 convert_element_type.10
  3.2 0.1 lt.30
  3.3 0.8 copy.18
  4.1 0.9 reshape_squeeze.13
  5.0 0.1 constant_dynamic-slice_fusion
  5.1 0.1 copy.19
  5.2 0.6 pad_convert_fusion.cmat_ref
  5.8 0.3 bitcast_select_fusion
  6.1 1.0 pad.10.idx_ref
  7.1 2.5 %reshape.39 = bf16[128,4,2048]{2,1,0:T(4,128)(2,1)S(1)} reshape(bf16[1,128,4,16,128]{4,3,2,1,0:T(8,128)(2,1)} %param.6) | data formatting | bytes 4194304 | tf_op jit(solution)/shard_map/reshape;squeeze | solution.py:249
  9.7 0.0 copy-start
  9.7 2.5 %copy.22 = bf16[128,4,2048]{2,0,1:T(8,128)(2,1)} copy(bf16[128,4,2048]{2,1,0:T(4,128)(2,1)S(1)} %reshape.39) | data formatting | bytes 4194304 | tf_op jit(solution)/shard_map/reshape;squeeze | solution.py:249
  12.1 0.0 copy-done
  12.1 2.7 %copy.13 = bf16[4,24,8,18,128]{4,1,3,0,2:T(8,128)(2,1)} copy(bf16[4,24,8,18,128]{4,2,3,1,0:T(8,128)(2,1)S(1)} %bitcast.23) | data formatting | bytes 7077888 | tf_op jit(solution)/shard_map/reshape;squeeze | solution.py:250
  14.8 128.1 %shard_map.64 = bf16[4,128,2048]{2,1,0:T(8,128)(2,1)} custom-call(bf16[4,128,2048]{2,1,0:T(8,128)(2,1)} %bitcast.25, bf16[8,1728,128]{2,1,0:T(8,128)(2,1)} %bitcast.24, s32[1728,128]{1,0:T(8,128)} %pad.10.idx_ref, f32[24,384]{1,0:T(8,128)} %pad_convert_fusion.cmat_ref, f32[1,2048]{1,0:T(1,128)} %bitcast.28), custom_call_target="tpu_custom_call" | custom-call | flops 7247757312 | bytes 16777216 | tf_op jit(solution)/shard_map/pallas_call | solution.py:263
  142.9 2.2 %copy.20 = bf16[64,8,16,128]{3,2,1,0:T(8,128)(2,1)S(1)} copy(bf16[64,8,16,128]{3,1,2,0:T(8,128)(2,1)} %bitcast.26) | data formatting | bytes 4194304
  145.1 2.0 %copy.16 = bf16[1,128,4,16,128]{4,3,2,1,0:T(8,128)(2,1)} copy(bf16[1,128,4,16,128]{4,3,1,2,0:T(8,128)(2,1)S(1)} %bitcast.22) | data formatting | bytes 4194304 | tf_op jit(solution)/shard_map/reshape | solution.py:289
  (1 shorter events, 0.0 us)
Async XLA Ops:
  9.7 2.5 %copy-start = (bf16[1,1,96,8,18,128]{5,3,4,2,1,0:T(8,128)(2,1)S(1)}, bf16[1,1,96,8,18,128]{5,3,4,2,1,0:T(8,128)(2,1)}, u32[]{:S(2)}) copy-start(bf16[1,1,96,8,18,128]{5,3,4,2,1,0:T(8,128)(2,1)} %param.7) | copy-start | bytes 10616836

commit v2 on v1

--- a/solution.py
+++ b/solution.py
@@ -70,20 +70,23 @@
             send_sem=(ag_send_r if right else ag_send_l).at[c, o], recv_sem=ag_recv.at[c, o],
             device_id={"slab": s + 1 if right else s - 1}, device_id_type=MESH)
 
+    order = [0, 2, 3, 1] if NCH == 4 else list(range(NCH))
+    late = range(3 * gpc, G) if NCH == 4 else range(0)
     for d in range(1, G):
-        psi_copy(d).start()
+        if d not in late:
+            psi_copy(d).start()
     psir[0] = psi_ref[g]
 
     def build(t, carry):
         at = pl.ds(pl.multiple_of(t * 16, 16), 16)
         where_to = idx_ref[at, :]
-        slots = [jnp.broadcast_to(where_to[:, j:j + 1], (16, 128)) for j in range(SL)]
-        values = [proj_ref[j, at, :].astype(jnp.float32) for j in range(SL)]
+        slots = [jnp.broadcast_to(where_to[:, j:j + 1], (16, 128)).astype(jnp.bfloat16) for j in range(SL)]
+        values = [proj_ref[j, at, :] for j in range(SL)]
         for b in range(NB):
-            acc = jnp.zeros((16, 128), jnp.float32)
+            acc = jnp.zeros((16, 128), jnp.bfloat16)
             for j in range(SL):
-                acc = jnp.where(slots[j] == b, values[j], acc)
-            table[at, b * 128:(b + 1) * 128] = acc.astype(jnp.bfloat16)
+                acc = jnp.where(slots[j] == jnp.bfloat16(b), values[j], acc)
+            table[at, b * 128:(b + 1) * 128] = acc
         return carry
 
     lax.fori_loop(0, rows // 16, build, 0)
@@ -107,35 +110,48 @@
 
         lax.fori_loop(0, S, one, 0)
 
+    def start_ends(c):
         @pl.when(s == 0)
         def _():
-            for o in range(S - 1, 0, -1):
-                rs_copy(c, o, True).start()
+            rs_copy(c, S - 1, True).start()
 
         @pl.when(s == S - 1)
         def _():
-            for o in range(S - 1):
-                rs_copy(c, o, False).start()
+            rs_copy(c, 0, False).start()
 
     def add_in(c, o, box):
         part[c, o] = (part[c, o].astype(jnp.float32) + box[c, o].astype(jnp.float32)).astype(jnp.bfloat16)
 
-    def reduce_on(c):
-        for i in range(S - 2):
-            o = S - 1 - i
-
-            @pl.when((s > 0) & (s < o))
+    def reduce_hop(c, tick):
+        @pl.when(s <= tick)
+        def _():
+            o = S - 1 - tick + s
+
+            @pl.when(s > 0)
             def _():
                 rs_copy(c, o, True).wait_recv()
                 add_in(c, o, from_left)
-                rs_copy(c, o, True).start()
-
-            @pl.when((s < S - 1) & (s > i))
-            def _():
-                rs_copy(c, i, False).wait_recv()
-                add_in(c, i, from_right)
-                rs_copy(c, i, False).start()
-
+
+            @pl.when(s < tick)
+            def _():
+                rs_copy(c, o + 1, True).wait_send()
+            rs_copy(c, o, True).start()
+
+        @pl.when(S - 1 - s <= tick)
+        def _():
+            o = tick - (S - 1 - s)
+
+            @pl.when(s < S - 1)
+            def _():
+                rs_copy(c, o, False).wait_recv()
+                add_in(c, o, from_right)
+
+            @pl.when(S - 1 - s < tick)
+            def _():
+                rs_copy(c, o - 1, False).wait_send()
+            rs_copy(c, o, False).start()
+
+    def finish(c):
         @pl.when(s > 0)
         def _():
             rs_copy(c, s, True).wait_recv()
@@ -164,23 +180,22 @@
         def _():
             ag_copy(c, s, False).start()
 
-    def gather_on(c):
-        for i in range(1, S):
-            @pl.when(s - i >= 0)
-            def _():
-                ag_copy(c, s - i, True).wait_recv()
-
-                @pl.when(s < S - 1)
-                def _():
-                    ag_copy(c, s - i, True).start()
-
-            @pl.when(s + i < S)
-            def _():
-                ag_copy(c, s + i, False).wait_recv()
-
-                @pl.when(s > 0)
-                def _():
-                    ag_copy(c, s + i, False).start()
+    def gather_hop(c, i):
+        @pl.when(s - i >= 0)
+        def _():
+            ag_copy(c, s - i, True).wait_recv()
+
+            @pl.when(s < S - 1)
+            def _():
+                ag_copy(c, s - i, True).start()
+
+        @pl.when(s + i < S)
+        def _():
+            ag_copy(c, s + i, False).wait_recv()
+
+            @pl.when(s > 0)
+            def _():
+                ag_copy(c, s + i, False).start()
 
     def apply(c):
         flipped[...] = coupled[c].reshape(rows, width).T
@@ -190,7 +205,7 @@
             at = pl.ds(pl.multiple_of(q * step, step), step)
             psi = psir[c * gpc:(c + 1) * gpc, :, at].reshape(width, step)
             value = jnp.dot(flipped[...], table[:, at], preferred_element_type=jnp.float32)
-            value += pot_ref[:, at] * psi.astype(jnp.float32)
+            value += pot_ref[:, at].astype(jnp.float32) * psi.astype(jnp.float32)
             value = value.astype(jnp.bfloat16).reshape(gpc, m, step)
             res[c * gpc:(c + 1) * gpc, :, at] = value
             return carry
@@ -202,28 +217,40 @@
             else:
                 out_ref[g] = res[0]
 
-    project(0)
-    if NCH > 1:
-        project(1)
+    project(order[0])
+    start_ends(order[0])
+    for d in late:
+        psi_copy(d - gpc).wait_send()
+        psi_copy(d).start()
+    for n in range(1, min(2, NCH)):
+        project(order[n])
     for ij in range(NP * NP):
         cwide[ij] = jnp.broadcast_to(cmat_ref[:, ij:ij + 1], (AIN, width))
-    for c in range(NCH):
-        reduce_on(c)
-        if c >= 1:
-            if c + 1 < NCH:
-                project(c + 1)
-            gather_on(c - 1)
-            apply(c - 1)
-    gather_on(NCH - 1)
-    apply(NCH - 1)
+    for n in range(NCH):
+        for i in range(S - 1):
+            if i > 0:
+                reduce_hop(order[n], i)
+            if n >= 1:
+                gather_hop(order[n - 1], i + 1)
+        if n + 1 < NCH:
+            start_ends(order[n + 1])
+        finish(order[n])
+        if n >= 1:
+            apply(order[n - 1])
+        if n + 2 < NCH:
+            project(order[n + 2])
+    for i in range(1, S):
+        gather_hop(order[NCH - 1], i)
+    apply(order[NCH - 1])
 
     for d in range(1, G):
-        psi_copy(d).wait_send()
+        if d + gpc not in late:
+            psi_copy(d).wait_send()
         out_copy(d).wait_send()
         out_copy(d).wait_recv()
     for c in range(NCH):
         for o in range(S):
-            @pl.when(s != o)
+            @pl.when((s == o - 1) | (s == o + 1))
             def _():
                 rs_copy(c, o, True).wait_send()
 
@@ -252,10 +279,10 @@
     used = jnp.arange(NP, dtype=jnp.int32)[None, :, None, None] < proj_counts[0].reshape(S, 1, own, 1)
     idx = jnp.where(used, block_index[0, 0].reshape(S, 1, own, SL), -1)
     idx = jnp.pad(idx, ((0, 0), (0, 0), (0, AIN - own), (0, 0)), constant_values=-1).reshape(rows, SL)
-    idx = jnp.pad(idx, ((0, 0), (0, 128 - SL)), constant_values=-1)
+    idx = jnp.pad(idx, ((0, 0), (0, 128 - SL)), constant_values=-1).astype(jnp.float32)
     cmat = lax.dynamic_slice_in_dim(coupling[0].reshape(AT, NP * NP), s * own, own, 0).astype(jnp.float32)
     cmat = jnp.pad(cmat, ((0, AIN - own), (0, (-NP * NP) % 128)))
-    pot = potential.reshape(1, NB * cells).astype(jnp.float32)
+    pot = potential.reshape(1, NB * cells)
     bf = jnp.bfloat16
     rows_o = NP * AIN
     dma = pltpu.SemaphoreType.DMA

time: 147 us -> 119 us (0.81)
  Pallas kernels: 128 us -> 100 us
    pallas_call x1, Pallas kernels: 128 us -> 100 us  [on_device(): pl.pallas_call(functools.partial(kernel, (G, S, NP, AIN, SL, NB, NCH, m))...]
    unnamed x5 -> x6, local copies, waits for them, and re-layouts: 2.8 us -> 4.08 us
where the time goes in v2:
time: 119 us
  Pallas kernels  100 us (84%)
  local copies, waits for them, and re-layouts  15.7 us (13%)
  other arithmetic  3.24 us (3%)
    pallas_call x1, Pallas kernels, on_device(): pl.pallas_call(functools.partial(kernel, (G, S, NP, AIN, SL, NB, NCH, m))...  100 us
    another operation x2, local copies, waits for them, and re-layouts, on_device(): wavefunctions[0].reshape(m, regions, NB * cells)  5.01 us
    unnamed x6, local copies, waits for them, and re-layouts  4.08 us
    another operation x1, local copies, waits for them, and re-layouts, on_device(): projectors[0, 0].reshape(S, own, SL, NP, cells).transpose(2, 0, 3, 1, 4)  2.67 us

profile of v2, /device:TPU:0, one launch (start us, length us, event | category | flops | bytes accessed | tf_op | source)
XLA Modules:
  0.0 119.1 jit_solution(2233593127423316037)
XLA Ops:
  0.0 0.5 broadcast.21
  0.5 1.3 %reduce.3 = s32[96]{0:T(128)S(1)} reduce(s32[1,96]{1,0:T(1,128)} %param.9, s32[]{:T(128)} %broadcast.21), dimensions={0}, to_apply=%param.9.reduce_sub_computation.3 | reduce | bytes 772 | tf_op args[3]
  1.8 0.1 lt.27
  1.9 1.3 %copy.25 = bf16[1,1,16,128]{3,1,2,0:T(2,128)(2,1)} copy(bf16[1,1,16,128]{3,2,1,0:T(8,128)(2,1)} %bitcast.32) | data formatting | bytes 8192
  3.2 0.1 lt.30
  3.3 0.8 copy.18
  4.1 0.9 reshape_squeeze.13
  5.0 0.1 constant_dynamic-slice_fusion
  5.1 0.1 copy.19
  5.2 0.6 pad_convert_fusion.1.cmat_ref
  5.8 0.3 bitcast_select_fusion
  6.1 1.0 pad_convert_fusion.idx_ref
  7.1 2.5 %reshape.27 = bf16[128,4,2048]{2,1,0:T(4,128)(2,1)S(1)} reshape(bf16[1,128,4,16,128]{4,3,2,1,0:T(8,128)(2,1)} %param.6) | data formatting | bytes 4194304 | tf_op jit(solution)/shard_map/reshape;squeeze | solution.py:276
  9.7 0.0 copy-start
  9.7 2.5 %copy.24 = bf16[128,4,2048]{2,0,1:T(8,128)(2,1)} copy(bf16[128,4,2048]{2,1,0:T(4,128)(2,1)S(1)} %reshape.27) | data formatting | bytes 4194304 | tf_op jit(solution)/shard_map/reshape;squeeze | solution.py:276
  12.2 0.0 copy-done
  12.2 2.7 %copy.13 = bf16[4,24,8,18,128]{4,1,3,0,2:T(8,128)(2,1)} copy(bf16[4,24,8,18,128]{4,2,3,1,0:T(8,128)(2,1)S(1)} %bitcast.26) | data formatting | bytes 7077888 | tf_op jit(solution)/shard_map/reshape;squeeze | solution.py:277
  14.8 100.1 %shard_map.64 = bf16[4,128,2048]{2,1,0:T(8,128)(2,1)} custom-call(bf16[4,128,2048]{2,1,0:T(8,128)(2,1)} %bitcast.28, bf16[8,1728,128]{2,1,0:T(8,128)(2,1)} %bitcast.27, f32[1728,128]{1,0:T(8,128)} %pad_convert_fusion.idx_ref, f32[24,384]{1,0:T(8,128)} %pad_convert_fusion.1.cmat_ref, bf16[1,2048]{1,0:T(2,128)(2,1)} %bitcast.31), custom_call_target="tpu_custom_call" | custom-call | flops 7247757312 | bytes 16777216 | tf_op jit(solution)/shard_map/pallas_call | solution.py:290
  114.9 2.2 %copy.21 = bf16[64,8,16,128]{3,2,1,0:T(8,128)(2,1)S(1)} copy(bf16[64,8,16,128]{3,1,2,0:T(8,128)(2,1)} %bitcast.29) | data formatting | bytes 4194304
  117.2 2.0 %copy.16 = bf16[1,128,4,16,128]{4,3,2,1,0:T(8,128)(2,1)} copy(bf16[1,128,4,16,128]{4,3,1,2,0:T(8,128)(2,1)S(1)} %bitcast.25) | data formatting | bytes 4194304 | tf_op jit(solution)/shard_map/reshape | solution.py:316
  (1 shorter events, 0.0 us)
Async XLA Ops:
  9.7 2.5 %copy-start = (bf16[1,1,96,8,18,128]{5,3,4,2,1,0:T(8,128)(2,1)S(1)}, bf16[1,1,96,8,18,128]{5,3,4,2,1,0:T(8,128)(2,1)}, u32[]{:S(2)}) copy-start(bf16[1,1,96,8,18,128]{5,3,4,2,1,0:T(8,128)(2,1)} %param.7) | copy-start | bytes 10616836

commit v3 on v2

--- a/solution.py
+++ b/solution.py
@@ -89,7 +89,7 @@
             table[at, b * 128:(b + 1) * 128] = acc
         return carry
 
-    lax.fori_loop(0, rows // 16, build, 0)
+    lax.fori_loop(0, rows // 16, build, 0, unroll=4)
 
     def project(c):
         for d in range(c * gpc, (c + 1) * gpc):

time: 119 us -> 117 us (0.983)
  Pallas kernels: 100 us -> 98.1 us
    pallas_call x1, Pallas kernels: 100 us -> 98.1 us  [on_device(): pl.pallas_call(functools.partial(kernel, (G, S, NP, AIN, SL, NB, NCH, m))...]
where the time goes in v3:
time: 117 us
  Pallas kernels  98.1 us (84%)
  local copies, waits for them, and re-layouts  15.7 us (13%)
  other arithmetic  3.24 us (3%)
    pallas_call x1, Pallas kernels, on_device(): pl.pallas_call(functools.partial(kernel, (G, S, NP, AIN, SL, NB, NCH, m))...  98.1 us
    another operation x2, local copies, waits for them, and re-layouts, on_device(): wavefunctions[0].reshape(m, regions, NB * cells)  5.01 us
    unnamed x6, local copies, waits for them, and re-layouts  4.08 us
    another operation x1, local copies, waits for them, and re-layouts, on_device(): projectors[0, 0].reshape(S, own, SL, NP, cells).transpose(2, 0, 3, 1, 4)  2.67 us

profile of v3, /device:TPU:0, one launch (start us, length us, event | category | flops | bytes accessed | tf_op | source)
XLA Modules:
  0.0 117.1 jit_solution(10632050043589876818)
XLA Ops:
  0.0 0.5 broadcast.21
  0.5 1.3 %reduce.3 = s32[96]{0:T(128)S(1)} reduce(s32[1,96]{1,0:T(1,128)} %param.9, s32[]{:T(128)} %broadcast.21), dimensions={0}, to_apply=%param.9.reduce_sub_computation.3 | reduce | bytes 772 | tf_op args[3]
  1.8 0.1 lt.27
  1.9 1.3 %copy.25 = bf16[1,1,16,128]{3,1,2,0:T(2,128)(2,1)} copy(bf16[1,1,16,128]{3,2,1,0:T(8,128)(2,1)} %bitcast.32) | data formatting | bytes 8192
  3.2 0.1 lt.30
  3.3 0.8 copy.18
  4.1 0.9 reshape_squeeze.13
  5.0 0.1 constant_dynamic-slice_fusion
  5.1 0.1 copy.19
  5.2 0.6 pad_convert_fusion.1.cmat_ref
  5.8 0.3 bitcast_select_fusion
  6.1 1.0 pad_convert_fusion.idx_ref
  7.1 2.5 %reshape.27 = bf16[128,4,2048]{2,1,0:T(4,128)(2,1)S(1)} reshape(bf16[1,128,4,16,128]{4,3,2,1,0:T(8,128)(2,1)} %param.6) | data formatting | bytes 4194304 | tf_op jit(solution)/shard_map/reshape;squeeze | solution.py:276
  9.7 0.0 copy-start
  9.7 2.5 %copy.24 = bf16[128,4,2048]{2,0,1:T(8,128)(2,1)} copy(bf16[128,4,2048]{2,1,0:T(4,128)(2,1)S(1)} %reshape.27) | data formatting | bytes 4194304 | tf_op jit(solution)/shard_map/reshape;squeeze | solution.py:276
  12.2 0.0 copy-done
  12.2 2.7 %copy.13 = bf16[4,24,8,18,128]{4,1,3,0,2:T(8,128)(2,1)} copy(bf16[4,24,8,18,128]{4,2,3,1,0:T(8,128)(2,1)S(1)} %bitcast.26) | data formatting | bytes 7077888 | tf_op jit(solution)/shard_map/reshape;squeeze | solution.py:277
  14.8 98.1 %shard_map.64 = bf16[4,128,2048]{2,1,0:T(8,128)(2,1)} custom-call(bf16[4,128,2048]{2,1,0:T(8,128)(2,1)} %bitcast.28, bf16[8,1728,128]{2,1,0:T(8,128)(2,1)} %bitcast.27, f32[1728,128]{1,0:T(8,128)} %pad_convert_fusion.idx_ref, f32[24,384]{1,0:T(8,128)} %pad_convert_fusion.1.cmat_ref, bf16[1,2048]{1,0:T(2,128)(2,1)} %bitcast.31), custom_call_target="tpu_custom_call" | custom-call | flops 7247757312 | bytes 16777216 | tf_op jit(solution)/shard_map/pallas_call | solution.py:290
  112.9 2.2 %copy.21 = bf16[64,8,16,128]{3,2,1,0:T(8,128)(2,1)S(1)} copy(bf16[64,8,16,128]{3,1,2,0:T(8,128)(2,1)} %bitcast.29) | data formatting | bytes 4194304
  115.1 2.0 %copy.16 = bf16[1,128,4,16,128]{4,3,2,1,0:T(8,128)(2,1)} copy(bf16[1,128,4,16,128]{4,3,1,2,0:T(8,128)(2,1)S(1)} %bitcast.25) | data formatting | bytes 4194304 | tf_op jit(solution)/shard_map/reshape | solution.py:316
  (1 shorter events, 0.0 us)
Async XLA Ops:
  9.7 2.5 %copy-start = (bf16[1,1,96,8,18,128]{5,3,4,2,1,0:T(8,128)(2,1)S(1)}, bf16[1,1,96,8,18,128]{5,3,4,2,1,0:T(8,128)(2,1)}, u32[]{:S(2)}) copy-start(bf16[1,1,96,8,18,128]{5,3,4,2,1,0:T(8,128)(2,1)} %param.7) | copy-start | bytes 10616836
